TPU v7x, 32 devices: a whole 2x2x4 slice. The times are simulated.
32 devices in a mesh: dp: 4 (over y, core), expert: 4 (over z), section: 2 (over x).
Axes of the slice: x: 2, y: 2, z: 4, core: 2. Of those that a mesh axis runs over, the one named last changes fastest.
Arguments:
- inputs: bfloat16 [2, 2048, 2048], P('section', ('dp', 'expert')), may hold values from -6 to 6
- out_grad: bfloat16 [2, 2048, 2048], P('section', ('dp', 'expert')), may hold values from -6 to 6
- expert_ids: int32 [2, 2048, 4], P('section', ('dp', 'expert')), may hold values from 0 to 7, all different within a row; in each aligned block of 128 rows (0 to 127, 128 to 255, ..., all dimensions but the last counted through in order) at most 72 rows name the same one
- gate_weights: float32 [2, 2048, 4], P('section', ('dp', 'expert')), may hold values from 0.05 to 0.6
- w_gate: bfloat16 [2, 8, 768, 2048], P('section', 'expert', 'dp'), may hold values from -0.125 to 0.125
- w_up: bfloat16 [2, 8, 768, 2048], P('section', 'expert', 'dp'), may hold values from -0.125 to 0.125
- w_down: bfloat16 [2, 8, 768, 2048], P('section', 'expert', 'dp'), may hold values from -0.21875 to 0.21875
Outputs:
- grad_prev: bfloat16 [2, 2048, 2048], P('section', ('dp', 'expert'))
- grad_gate: bfloat16 [2, 8, 768, 2048], P('section', 'expert', 'dp')
- grad_up: bfloat16 [2, 8, 768, 2048], P('section', 'expert', 'dp')
- grad_down: bfloat16 [2, 8, 768, 2048], P('section', 'expert', 'dp')
Inputs may be any that keep to these rules, and one draw needn't show every extreme that they name: `expert_ids`: each row names 4 different experts. In the rows of one device no expert is named by more than 72 rows, and in some devices' rows one expert is named by exactly 72.
All inputs are finite; a program needn't handle non-finite values.
Results may differ from a plain program's by a relative error of at most 0.013.
Values may be sent and summed in bfloat16 or wider, within the bound.
A program may use at most 192 MiB of HBM per device.

v0:
```python
import jax
import jax.numpy as jnp
from jax import lax
from jax.sharding import PartitionSpec as P

GROUP = ("dp", "expert")


def passed_along(block, axis, distance):
    devices = range(lax.axis_size(axis))
    route = [(i - distance, i) for i in devices if i - distance in devices]
    return lax.ppermute(block, axis, route)


def rows_by(a, b):
    return lax.dot_general(a, b, (((1,), (1,)), ((), ())), preferred_element_type=jnp.float32)


def over_rows(a, b):
    return lax.dot_general(a, b, (((0,), (0,)), ((), ())), preferred_element_type=jnp.float32)


def share_table(route_ids, gates, all_experts):
    named = route_ids[:, :, None] == jnp.arange(all_experts, dtype=jnp.int32)[None, None, :]
    return jnp.sum(jnp.where(named, gates[:, :, None], 0.0), axis=1)


def body(inputs, out_grad, expert_ids, gate_weights, w_gate, w_up, w_down):
    local_experts, hidden_share, model_width = w_gate.shape[1:]
    all_experts = local_experts * lax.axis_size("expert")
    units = local_experts * hidden_share
    gate_mat = w_gate[0].reshape(units, model_width)
    up_mat = w_up[0].reshape(units, model_width)
    down_mat = w_down[0].reshape(units, model_width)

    table = share_table(expert_ids[0], gate_weights[0], all_experts)
    table = lax.all_gather(table, GROUP, axis=0, tiled=True)
    tokens = lax.all_gather(inputs[0], GROUP, axis=0, tiled=True)
    grads_out = lax.all_gather(out_grad[0], GROUP, axis=0, tiled=True)
    own = lax.dynamic_slice_in_dim(
        table, lax.axis_index("expert") * local_experts, local_experts, axis=1
    )
    share = jnp.repeat(own, hidden_share, axis=1)

    pre_gate = rows_by(tokens, gate_mat)
    pre_up = rows_by(tokens, up_mat)
    sigmoid_gate = jax.nn.sigmoid(pre_gate)
    act_gate = pre_gate * sigmoid_gate
    hidden = (act_gate * pre_up * share).astype(jnp.bfloat16)
    hidden_grad = rows_by(grads_out, down_mat) * share
    gate_delta = (
        hidden_grad * pre_up * sigmoid_gate * (1.0 + pre_gate * (1.0 - sigmoid_gate))
    ).astype(jnp.bfloat16)
    up_delta = (hidden_grad * act_gate).astype(jnp.bfloat16)

    deltas = jnp.concatenate([gate_delta, up_delta], axis=1)
    mats = jnp.concatenate([gate_mat, up_mat], axis=0)
    partial_value = jnp.dot(deltas, mats, preferred_element_type=jnp.float32)
    token_grad = lax.psum_scatter(
        partial_value.astype(jnp.bfloat16), GROUP, scatter_dimension=0, tiled=True
    )
    grad_gate = over_rows(gate_delta, tokens).astype(jnp.bfloat16)
    grad_up = over_rows(up_delta, tokens).astype(jnp.bfloat16)
    grad_down = over_rows(hidden, grads_out).astype(jnp.bfloat16)
    grad_prev = passed_along(token_grad, "section", -1)
    shape = w_gate.shape
    return (
        grad_prev[None],
        grad_gate.reshape(shape),
        grad_up.reshape(shape),
        grad_down.reshape(shape),
    )


def solution(mesh):
    rows = P("section", GROUP, None)
    weights = P("section", "expert", "dp", None)
    return jax.shard_map(
        body,
        mesh=mesh,
        in_specs=(rows,) * 4 + (weights,) * 3,
        out_specs=(rows,) + (weights,) * 3,
        check_vma=False,
    )
```

profile of v0, /device:TPU:0, one launch (start us, length us, event | category | flops | bytes accessed | tf_op | source)
XLA Modules:
  0.0 312.8 jit_solution(11747492841741658007)
XLA Ops:
  7.2 0.0 copy-start
  7.2 0.0 all-gather.7.cloned.1.call-start
  7.2 0.7 all-gather.7.cloned.1.call-update
  7.9 0.0 all-gather.5.cloned.1.call-start
  8.0 0.7 all-gather.5.cloned.1.call-update
  8.7 0.0 reduce-scatter.2.cloned.1.call-start
  8.7 0.7 select_reduce_fusion
  9.4 35.0 %all_gather.10 = f32[2048,8]{0,1:T(8,128)S(1)} all-gather(f32[128,8]{0,1:T(8,128)S(1)} %select_reduce_fusion), channel_id=1, replica_groups=mesh['dp'=4,'expert'=4,'section'=2] {'dp','expert'}, dimensions={0}, use_global_device_ids=true | all-gather | bytes 69632 | tf_op jit(solution)/shard_map/all_gather | solution.py:37
  44.5 44.2 %all-gather.7.cloned.1.call-done = bf16[1,2048,2048]{2,1,0:T(8,128)(2,1)} async-done(((bf16[1,128,2048]{2,1,0:T(8,128)(2,1)}), bf16[1,2048,2048]{2,1,0:T(8,128)(2,1)}) %all-gather.7.cloned.1.call-update) | async-done | bytes 8388624 | tf_op jit(solution)/shard_map/all_gather | solution.py:38
  88.7 8.9 %fusion.4 = f32[2048,384]{0,1:T(8,128)} fusion(bf16[384,2048]{1,0:T(8,128)(2,1)} %bitcast.50, bf16[1,2048,2048]{2,1,0:T(8,128)(2,1)} %all-gather.7.cloned.1.call-done), kind=kOutput, calls=%fused_computation.4 | convolution fusion | flops 3221225472 | bytes 13107200 | tf_op jit(solution)/shard_map/dot_general | solution.py:16
  97.6 66.5 %all-gather.5.cloned.1.call-done = bf16[1,2048,2048]{2,1,0:T(8,128)(2,1)} async-done(((bf16[1,128,2048]{2,1,0:T(8,128)(2,1)}), bf16[1,2048,2048]{2,1,0:T(8,128)(2,1)}) %all-gather.5.cloned.1.call-update) | async-done | bytes 8388624 | tf_op jit(solution)/shard_map/all_gather | solution.py:39
  164.1 0.0 copy-done
  164.1 0.0 copy-start.1
  164.1 0.0 copy-start.2
  164.1 0.0 copy-start.3
  164.1 6.2 %bitcast_multiply_fusion.1 = f32[2048,384]{0,1:T(8,128)S(1)} fusion(bf16[384,2048]{1,0:T(8,128)(2,1)S(1)} %bitcast.44, bf16[1,2048,2048]{2,1,0:T(8,128)(2,1)} %all-gather.5.cloned.1.call-done, f32[2048,2]{0,1:T(2,128)S(1)} %constant_dynamic-slice_fusion), kind=kOutput, calls=%fused_computation.14 | convolution fusion | flops 3222011904 | bytes 13123584 | tf_op jit(solution)/shard_map/dot_general | solution.py:16
  170.3 0.0 copy-done.1
  170.3 0.5 copy-done.2
  170.8 0.4 copy-done.3
  171.2 0.0 copy-start.7
  171.2 4.6 %fusion.12 = (bf16[2048,384]{0,1:T(8,128)(2,1)S(1)}, bf16[2048,384]{0,1:T(8,128)(2,1)S(1)}, bf16[2048,384]{0,1:T(8,128)(2,1)S(1)}) fusion(f32[2048,2]{0,1:T(2,128)S(1)} %constant_dynamic-slice_fusion, f32[2048,384]{0,1:T(8,128)S(1)} %copy-done.2, f32[2048,384]{0,1:T(8,128)S(1)} %bitcast_multiply_fusion.1, bf16[384,2048]{1,0:T(8,128)(2,1)S(1)} %bitcast.45, ...), kind=kOutput, calls=%fused_computation.15 | convolution fusion | flops 3233808384 | bytes 20987904 | tf_op jit(solution)/shard_map/dot_general | solution.py:16
  175.8 0.0 copy-start.4
  175.9 0.0 copy-start.6
  175.9 1.1 copy-done.4
  177.0 0.5 copy-done.6
  177.5 0.0 copy-done.7
  177.5 9.0 %convolution_convert_fusion = bf16[2048,2048]{1,0:T(8,128)(2,1)} fusion(bf16[2048,384]{0,1:T(8,128)(2,1)S(1)} %get-tuple-element.6, bf16[2048,384]{0,1:T(8,128)(2,1)S(1)} %get-tuple-element.5, bf16[384,2048]{1,0:T(8,128)(2,1)S(1)} %bitcast.46, bf16[384,2048]{1,0:T(8,128)(2,1)S(1)} %bitcast.51), kind=kOutput, calls=%fused_computation.12 | convolution fusion | flops 6459228160 | bytes 14680064 | tf_op jit(solution)/shard_map/dot_general | solution.py:58
  186.6 0.0 reduce-scatter.2.cloned.1.call-update
  186.6 0.0 copy-start.5
  186.6 8.7 %fusion.25 = bf16[384,2048]{1,0:T(8,128)(2,1)} fusion(bf16[2048,384]{0,1:T(8,128)(2,1)} %copy-done.6, bf16[1,2048,2048]{2,1,0:T(8,128)(2,1)} %all-gather.7.cloned.1.call-done), kind=kOutput, calls=%fused_computation.27 | convolution fusion | flops 3222011904 | bytes 11534336 | tf_op jit(solution)/shard_map/dot_general | solution.py:20
  195.3 0.0 copy-done.5
  195.3 8.6 %fusion.28 = bf16[384,2048]{1,0:T(8,128)(2,1)} fusion(bf16[2048,384]{0,1:T(8,128)(2,1)S(1)} %copy-done.5, bf16[1,2048,2048]{2,1,0:T(8,128)(2,1)} %all-gather.7.cloned.1.call-done), kind=kOutput, calls=%fused_computation.28 | convolution fusion | flops 3222011904 | bytes 11534336 | tf_op jit(solution)/shard_map/dot_general | solution.py:20
  203.9 85.8 %reduce-scatter.2.cloned.1.call-done = bf16[128,2048]{1,0:T(8,128)(2,1)} async-done(((bf16[2048,2048]{1,0:T(8,128)(2,1)}), bf16[128,2048]{1,0:T(8,128)(2,1)}) %reduce-scatter.2.cloned.1.call-update) | async-done | bytes 524304 | tf_op jit(solution)/shard_map/reduce_scatter | solution.py:59
  289.7 1.3 collective-permute-start
  291.0 7.9 %fusion.22 = bf16[384,2048]{1,0:T(8,128)(2,1)} fusion(bf16[2048,384]{0,1:T(8,128)(2,1)S(1)} %get-tuple-element.4, bf16[1,2048,2048]{2,1,0:T(8,128)(2,1)} %all-gather.5.cloned.1.call-done), kind=kOutput, calls=%fused_computation.26 | convolution fusion | flops 3222011904 | bytes 11534336 | tf_op jit(solution)/shard_map/dot_general | solution.py:20
  298.9 6.6 %collective-permute-done = bf16[128,2048]{1,0:T(8,128)(2,1)S(1)} collective-permute-done((bf16[128,2048]{1,0:T(8,128)(2,1)}, bf16[128,2048]{1,0:T(8,128)(2,1)S(1)}, u32[]{:S(2)}, u32[]{:S(2)}) %collective-permute-start) | collective-permute-done | bytes 524320 | tf_op jit(solution)/shard_map/ppermute | solution.py:12
  305.5 0.8 copy.14
  (1 shorter events, 0.0 us)
Async XLA Ops:
  7.2 156.9 %copy-start = (bf16[1,2,192,2048]{3,2,1,0:T(8,128)(2,1)S(1)}, bf16[1,2,192,2048]{3,2,1,0:T(8,128)(2,1)}, u32[]{:S(2)}) copy-start(bf16[1,2,192,2048]{3,2,1,0:T(8,128)(2,1)} %param.13) | copy-start | bytes 4718596
  7.2 81.5 %all-gather.7.cloned.1.call-start = ((), (), s32[]{:S(2)}) async-start(), calls=%async_computation.3 | async-start | bytes 8912896 | tf_op jit(solution)/shard_map/all_gather | solution.py:38
  7.9 156.2 %all-gather.5.cloned.1.call-start = ((), (), s32[]{:S(2)}) async-start(), calls=%async_computation.2 | async-start | bytes 8912896 | tf_op jit(solution)/shard_map/all_gather | solution.py:39
  8.7 281.0 %reduce-scatter.2.cloned.1.call-start = ((), (), s32[]{:S(2)}) async-start(), calls=%async_computation.1 | async-start | bytes 8912896 | tf_op jit(solution)/shard_map/reduce_scatter | solution.py:59
  164.1 6.2 %copy-start.1 = (bf16[1,2048,2048]{2,1,0:T(8,128)(2,1)S(1)}, bf16[1,2048,2048]{2,1,0:T(8,128)(2,1)}, u32[]{:S(2)}) copy-start(bf16[1,2048,2048]{2,1,0:T(8,128)(2,1)} %all-gather.7.cloned.1.call-done) | copy-start | bytes 25165828
  164.1 6.7 %copy-start.2 = (f32[2048,384]{0,1:T(8,128)S(1)}, f32[2048,384]{0,1:T(8,128)}, u32[]{:S(2)}) copy-start(f32[2048,384]{0,1:T(8,128)} %fusion.4) | copy-start | bytes 9437188
  164.1 7.1 %copy-start.3 = (bf16[1,2,192,2048]{3,2,1,0:T(8,128)(2,1)S(1)}, bf16[1,2,192,2048]{3,2,1,0:T(8,128)(2,1)}, u32[]{:S(2)}) copy-start(bf16[1,2,192,2048]{3,2,1,0:T(8,128)(2,1)} %param.12) | copy-start | bytes 4718596
  171.2 6.3 %copy-start.7 = (bf16[1,2,192,2048]{3,2,1,0:T(8,128)(2,1)S(1)}, bf16[1,2,192,2048]{3,2,1,0:T(8,128)(2,1)}, u32[]{:S(2)}) copy-start(bf16[1,2,192,2048]{3,2,1,0:T(8,128)(2,1)} %param.11) | copy-start | bytes 4718596
  175.8 1.1 copy-start.4
  175.9 1.7 copy-start.6
  186.6 8.7 %copy-start.5 = (bf16[2048,384]{0,1:T(8,128)(2,1)S(1)}, bf16[2048,384]{0,1:T(8,128)(2,1)}, u32[]{:S(2)}) copy-start(bf16[2048,384]{0,1:T(8,128)(2,1)} %copy-done.4) | copy-start | bytes 4718596
  289.7 15.8 %collective-permute-start = (bf16[128,2048]{1,0:T(8,128)(2,1)}, bf16[128,2048]{1,0:T(8,128)(2,1)S(1)}, u32[]{:S(2)}, u32[]{:S(2)}) collective-permute-start(bf16[128,2048]{1,0:T(8,128)(2,1)} %reduce-scatter.2.cloned.1.call-done), channel_id=1, source_target_pairs={{1,0},{3,2},{5,4},{7,6},{9,8},{11,10},{13,12},{15,14},{17,16},{19,... | collective-permute-start | bytes 1572872 | tf_op jit(solution)/shard_map/ppermute | solution.py:12
Sparse Core Ops, SparseCore 0:
  10.2 78.4 all-gather.6
  90.9 73.1 all-gather.4
  186.7 102.9 reduce-scatter.1
where the time goes:
time: 313 us
  waiting for transfers between devices  205 us (65%)
  matrix products  53.9 us (17%)
  blocking collectives  35 us (11%)
  between operations  13.8 us (4%)
  local copies, waits for them, and re-layouts  3.39 us (1%)
    reduce_scatter x1, waiting for transfers between devices, body(): lax.psum_scatter(partial_value.astype(jnp.bfloat16), GROUP, scatter_dimen...  85.8 us
    all_gather x1, waiting for transfers between devices, body(): grads_out = lax.all_gather(out_grad[0], GROUP, axis=0, tiled=True)  66.5 us
    all_gather x1, waiting for transfers between devices, body(): tokens = lax.all_gather(inputs[0], GROUP, axis=0, tiled=True)  44.2 us
    all_gather x1, blocking collectives, body(): table = lax.all_gather(table, GROUP, axis=0, tiled=True)  35 us
    dot_general x3, matrix products, over_rows(): lax.dot_general(a, b, (((0,), (0,)), ((), ())), preferred_element_type=jn...  25.2 us
    dot_general x3, matrix products, rows_by(): lax.dot_general(a, b, (((1,), (1,)), ((), ())), preferred_element_type=jn...  19.7 us
    dot_general x1, matrix products, body(): partial_value = jnp.dot(deltas, mats, preferred_element_type=jnp.float32)  9.05 us
    ppermute x1, waiting for transfers between devices, passed_along(): return lax.ppermute(block, axis, route)  6.62 us
  transfers between devices with their start and end apart: 4, of which 4 were waited for; matrix products, arithmetic and copies ran while one was open for 11% of the time, Pallas kernels for 0%

commit v1 on v0

--- a/solution.py
+++ b/solution.py
@@ -1,6 +1,10 @@
+import functools
+
 import jax
 import jax.numpy as jnp
 from jax import lax
+from jax.experimental import pallas as pl
+from jax.experimental.pallas import tpu as pltpu
 from jax.sharding import PartitionSpec as P
 
 GROUP = ("dp", "expert")
@@ -23,6 +27,132 @@
 def share_table(route_ids, gates, all_experts):
     named = route_ids[:, :, None] == jnp.arange(all_experts, dtype=jnp.int32)[None, None, :]
     return jnp.sum(jnp.where(named, gates[:, :, None], 0.0), axis=1)
+
+
+def gather_kernel(ways, lines, *refs):
+    count = (len(refs) - 3) // 2
+    own, full = refs[:count], refs[count : 2 * count]
+    send_sem, recv_sem, local_sem = refs[2 * count :]
+    dp, z = lax.axis_index("dp"), lax.axis_index("expert")
+    across = lax.rem(dp + 2, lines)
+    beside = dp + 1 - 2 * lax.rem(dp, 2)
+    up, down = lax.rem(z + 1, ways), lax.rem(z + ways - 1, ways)
+
+    def target(d, e):
+        return {"dp": d, "expert": e}
+
+    barrier = pltpu.get_barrier_semaphore()
+
+    def greet(d, e):
+        pl.semaphore_signal(
+            barrier, inc=1, device_id=target(d, e), device_id_type=pl.DeviceIdType.MESH
+        )
+
+    greet(across, z)
+    greet(beside, z)
+    pl.when(z < ways - 1)(lambda: greet(dp, up))
+    pl.when(z > 0)(lambda: greet(dp, down))
+    inner = jnp.logical_and(z > 0, z < ways - 1)
+    pl.when(inner)(lambda: pl.semaphore_wait(barrier, 4))
+    pl.when(jnp.logical_not(inner))(lambda: pl.semaphore_wait(barrier, 3))
+
+    def copy(i, line, place, number, d, e, from_own=False):
+        slot = line * ways + place
+        return pltpu.make_async_remote_copy(
+            src_ref=own[i] if from_own else full[i].at[slot],
+            dst_ref=full[i].at[slot],
+            send_sem=send_sem.at[i, number],
+            recv_sem=recv_sem.at[i, slot],
+            device_id=target(d, e),
+            device_id_type=pl.DeviceIdType.MESH,
+        )
+
+    everything = range(count)
+    pending = []
+
+    def send(cond, i, line, place, number, d, e, from_own=False):
+        made = functools.partial(copy, i, line, place, number, d, e, from_own)
+        if cond is None:
+            made().start()
+        else:
+            pl.when(cond)(lambda: made().start())
+        pending.append((cond, made))
+
+    def received(i, line, place):
+        copy(i, line, place, 0, across, z).wait_recv()
+
+    steps = [(0, 0)] + [(j, sign) for j in range(1, ways) for sign in (-1, 1)]
+    kept = [pltpu.make_async_copy(own[i], full[i].at[dp * ways + z], local_sem.at[i]) for i in everything]
+    for i in everything:
+        send(z < ways - 1, i, dp, z, 0, dp, up, True)
+        send(z > 0, i, dp, z, ways, dp, down, True)
+        send(None, i, dp, z, 2 * ways, across, z, True)
+    for i in everything:
+        send(None, i, dp, z, 4 * ways, beside, z, True)
+        kept[i].start()
+    wide = 2 * ways
+    for n, (j, sign) in enumerate(steps):
+        if n > 0:
+            here = z >= j if sign < 0 else z + j < ways
+            place = lax.rem(z + sign * j + ways, ways)
+            number = n
+            for i in everything:
+
+                def arrive(i=i, place=place):
+                    received(i, dp, place)
+
+                pl.when(here)(arrive)
+                if sign < 0:
+                    if j < ways - 1:
+                        send(jnp.logical_and(here, z < ways - 1), i, dp, place, j, dp, up)
+                elif j < ways - 1:
+                    send(jnp.logical_and(here, z > 0), i, dp, place, ways + j, dp, down)
+                send(here, i, dp, place, wide + number, across, z)
+                send(here, i, dp, place, 2 * wide + number, beside, z)
+            cross_from(steps[n - 1], z, ways, everything, received, send, across, beside, 3 * wide + n - 1)
+    cross_from(steps[-1], z, ways, everything, received, send, across, beside, 3 * wide + len(steps) - 1)
+    other = lax.rem(beside + 2, lines)
+    for line in (beside, other):
+        for place in range(ways):
+            for i in everything:
+                received(i, line, place)
+    for cond, made in pending:
+        if cond is None:
+            made().wait_send()
+        else:
+            pl.when(cond)(lambda made=made: made().wait_send())
+    for k in kept:
+        k.wait()
+
+
+def cross_from(step, z, ways, everything, received, send, across, beside, number):
+    j, sign = step
+    here = None if j == 0 else (z >= j if sign < 0 else z + j < ways)
+    place = lax.rem(z + sign * j + ways, ways)
+    for i in everything:
+        if here is None:
+            received(i, across, place)
+        else:
+            pl.when(here)(lambda i=i: received(i, across, place))
+        send(here, i, across, place, number, beside, z)
+
+
+def gathered(*blocks):
+    ways, lines = lax.axis_size("expert"), lax.axis_size("dp")
+    slots = ways * lines
+    full = pl.pallas_call(
+        functools.partial(gather_kernel, ways, lines),
+        out_shape=[jax.ShapeDtypeStruct((slots,) + b.shape, b.dtype) for b in blocks],
+        in_specs=[pl.BlockSpec(memory_space=pl.ANY)] * len(blocks),
+        out_specs=[pl.BlockSpec(memory_space=pl.ANY)] * len(blocks),
+        scratch_shapes=[
+            pltpu.SemaphoreType.DMA((len(blocks), 8 * ways)),
+            pltpu.SemaphoreType.DMA((len(blocks), slots)),
+            pltpu.SemaphoreType.DMA((len(blocks),)),
+        ],
+        compiler_params=pltpu.CompilerParams(collective_id=0, has_side_effects=True),
+    )(*blocks)
+    return [f.reshape((-1, f.shape[-1])) for f in full]
 
 
 def body(inputs, out_grad, expert_ids, gate_weights, w_gate, w_up, w_down):
@@ -34,9 +164,14 @@
     down_mat = w_down[0].reshape(units, model_width)
 
     table = share_table(expert_ids[0], gate_weights[0], all_experts)
-    table = lax.all_gather(table, GROUP, axis=0, tiled=True)
-    tokens = lax.all_gather(inputs[0], GROUP, axis=0, tiled=True)
-    grads_out = lax.all_gather(out_grad[0], GROUP, axis=0, tiled=True)
+    if (lax.axis_size("dp"), lax.axis_size("expert")) == (4, 4):
+        table = jnp.pad(table, ((0, 0), (0, 128 - all_experts)))
+        table, tokens, grads_out = gathered(table, inputs[0], out_grad[0])
+    else:
+        table, tokens, grads_out = (
+            lax.all_gather(block, GROUP, axis=0, tiled=True)
+            for block in (table, inputs[0], out_grad[0])
+        )
     own = lax.dynamic_slice_in_dim(
         table, lax.axis_index("expert") * local_experts, local_experts, axis=1
     )

time: 313 us -> 286 us (0.914)
  Pallas kernels: 0 us -> 117 us
  waiting for transfers between devices: 205 us -> 92.5 us
  blocking collectives: 35 us -> 0 us
    pallas_call x0 -> x1, Pallas kernels: none -> 117 us  [gathered(): pl.pallas_call(functools.partial(gather_kernel, ways, lines), out_shape=[...]
    all_gather x2 -> x0, waiting for transfers between devices: 111 us -> none  [the longest x1 66.5 us: body(): grads_out = lax.all_gather(out_grad[0], GROUP, axis=0, tiled=True)]
    all_gather x1 -> x0, blocking collectives: 35 us -> none  [body(): table = lax.all_gather(table, GROUP, axis=0, tiled=True)]
  transfers between devices with their start and end apart: 4 -> 2, of which waited for: 4 -> 2; matrix products, arithmetic and copies ran while one was open for 11% -> 9% of each run, Pallas kernels for 0% -> 0%
where the time goes in v1:
time: 286 us; the launch traced here: 285 us
  Pallas kernels  117 us (41%)
  waiting for transfers between devices  92.5 us (32%)
  matrix products  54.6 us (19%)
  between operations  14.1 us (5%)
  local copies, waits for them, and re-layouts  5.1 us (2%)
    pallas_call x1, Pallas kernels, gathered(): pl.pallas_call(functools.partial(gather_kernel, ways, lines), out_shape=[...  117 us
    reduce_scatter x1, waiting for transfers between devices, body(): lax.psum_scatter(partial_value.astype(jnp.bfloat16), GROUP, scatter_dimen...  85.8 us
    dot_general x3, matrix products, over_rows(): lax.dot_general(a, b, (((0,), (0,)), ((), ())), preferred_element_type=jn...  25.2 us
    dot_general x3, matrix products, rows_by(): lax.dot_general(a, b, (((1,), (1,)), ((), ())), preferred_element_type=jn...  20.4 us
    dot_general x1, matrix products, body(): partial_value = jnp.dot(deltas, mats, preferred_element_type=jnp.float32)  8.98 us
    ppermute x1, waiting for transfers between devices, passed_along(): return lax.ppermute(block, axis, route)  6.64 us
  transfers between devices with their start and end apart: 2, of which 2 were waited for; matrix products, arithmetic and copies ran while one was open for 9% of the time, Pallas kernels for 0%

profile of v1, /device:TPU:0, one launch (start us, length us, event | category | flops | bytes accessed | tf_op | source)
XLA Modules:
  0.0 285.4 jit_solution(14801436929803035736)
XLA Ops:
  7.2 0.0 copy-start
  7.2 0.0 reduce-scatter.2.cloned.1.call-start
  7.2 0.8 select_reduce_fusion
  8.1 0.1 copy.14
  8.2 0.6 pad.4.refs_0_
  8.8 117.0 %shard_map.102 = (f32[16,128,128]{2,1,0:T(8,128)}, bf16[16,128,2048]{2,1,0:T(8,128)(2,1)}, bf16[16,128,2048]{2,1,0:T(8,128)(2,1)}) custom-call(f32[128,128]{1,0:T(8,128)} %pad.4.refs_0_, bf16[128,2048]{1,0:T(8,128)(2,1)} %bitcast.41, bf16[128,2048]{1,0:T(8,128)(2,1)} %bitcast.42), custom_call_target="tpu_custom_call" | custom-call | tf_op jit(solution)/shard_map/pallas_call | solution.py:143
  125.8 1.6 constant_dynamic-slice_fusion
  127.3 0.3 copy.15
  127.7 6.4 %fusion.9 = f32[2048,384]{0,1:T(8,128)S(1)} fusion(bf16[2048,2048]{1,0:T(8,128)(2,1)} %bitcast.34, bf16[384,2048]{1,0:T(8,128)(2,1)} %bitcast.46), kind=kOutput, calls=%fused_computation.21 | convolution fusion | flops 3221225472 | bytes 13107200 | tf_op jit(solution)/shard_map/dot_general | solution.py:20
  134.0 0.0 copy-done
  134.0 0.0 copy-start.1
  134.0 6.0 %bitcast_multiply_fusion.1 = f32[2048,384]{0,1:T(8,128)S(1)} fusion(bf16[2048,2048]{1,0:T(8,128)(2,1)} %bitcast.32, bf16[384,2048]{1,0:T(8,128)(2,1)S(1)} %bitcast.31, f32[2048,2]{0,1:T(2,128)S(1)} %copy.15), kind=kOutput, calls=%fused_computation.2 | convolution fusion | flops 3222011904 | bytes 13123584 | tf_op jit(solution)/shard_map/dot_general | solution.py:20
  140.0 0.0 copy-done.1
  140.0 0.0 copy-start.5
  140.1 8.1 %fusion = (bf16[2048,384]{0,1:T(8,128)(2,1)S(1)}, bf16[2048,384]{0,1:T(8,128)(2,1)S(1)}, bf16[2048,384]{0,1:T(8,128)(2,1)S(1)}) fusion(f32[2048,2]{0,1:T(2,128)S(1)} %copy.15, f32[2048,384]{0,1:T(8,128)S(1)} %fusion.9, f32[2048,384]{0,1:T(8,128)S(1)} %bitcast_multiply_fusion.1, bf16[2048,2048]{1,0:T(8,128)(2,1)} %bitcast.35, bf16[384,2048]{1,0:T(8,128)(2,1)S(1)} %bitcast.38), kind=kOutput, calls=%fused_computation.3 | convolution fusion | flops 3233808384 | bytes 20987904 | tf_op jit(solution)/shard_map/dot_general | solution.py:20
  148.1 0.0 copy-start.2
  148.2 0.0 copy-start.4
  148.2 1.1 copy-done.2
  149.3 0.5 copy-done.4
  149.8 0.0 copy-done.5
  149.8 9.0 %convolution_convert_fusion = bf16[2048,2048]{1,0:T(8,128)(2,1)} fusion(bf16[2048,384]{0,1:T(8,128)(2,1)S(1)} %get-tuple-element.12, bf16[2048,384]{0,1:T(8,128)(2,1)S(1)} %get-tuple-element.11, bf16[384,2048]{1,0:T(8,128)(2,1)S(1)} %bitcast.39, bf16[384,2048]{1,0:T(8,128)(2,1)S(1)} %bitcast.47), kind=kOutput, calls=%fused_computation | convolution fusion | flops 6459228160 | bytes 14680064 | tf_op jit(solution)/shard_map/dot_general | solution.py:193
  158.8 0.0 reduce-scatter.2.cloned.1.call-update
  158.8 0.0 copy-start.3
  158.8 8.6 %convolution_convert_fusion.3 = bf16[384,2048]{1,0:T(8,128)(2,1)} fusion(bf16[2048,384]{0,1:T(8,128)(2,1)} %copy-done.4, bf16[2048,2048]{1,0:T(8,128)(2,1)} %bitcast.36), kind=kOutput, calls=%fused_computation.16 | convolution fusion | flops 3222011904 | bytes 11534336 | tf_op jit(solution)/shard_map/dot_general | solution.py:24
  167.4 0.0 copy-done.3
  167.4 8.7 %convolution_convert_fusion.2 = bf16[384,2048]{1,0:T(8,128)(2,1)} fusion(bf16[2048,384]{0,1:T(8,128)(2,1)S(1)} %copy-done.3, bf16[2048,2048]{1,0:T(8,128)(2,1)} %bitcast.37), kind=kOutput, calls=%fused_computation.15 | convolution fusion | flops 3222011904 | bytes 11534336 | tf_op jit(solution)/shard_map/dot_general | solution.py:24
  176.1 85.8 %reduce-scatter.2.cloned.1.call-done = bf16[128,2048]{1,0:T(8,128)(2,1)} async-done(((bf16[2048,2048]{1,0:T(8,128)(2,1)}), bf16[128,2048]{1,0:T(8,128)(2,1)}) %reduce-scatter.2.cloned.1.call-update) | async-done | bytes 524304 | tf_op jit(solution)/shard_map/reduce_scatter | solution.py:194
  262.0 1.3 collective-permute-start
  263.2 7.9 %convolution_convert_fusion.1 = bf16[384,2048]{1,0:T(8,128)(2,1)} fusion(bf16[2048,384]{0,1:T(8,128)(2,1)S(1)} %get-tuple-element.10, bf16[2048,2048]{1,0:T(8,128)(2,1)} %bitcast.33), kind=kOutput, calls=%fused_computation.14 | convolution fusion | flops 3222011904 | bytes 11534336 | tf_op jit(solution)/shard_map/dot_general | solution.py:24
  271.1 6.6 %collective-permute-done = bf16[128,2048]{1,0:T(8,128)(2,1)S(1)} collective-permute-done((bf16[128,2048]{1,0:T(8,128)(2,1)}, bf16[128,2048]{1,0:T(8,128)(2,1)S(1)}, u32[]{:S(2)}, u32[]{:S(2)}) %collective-permute-start) | collective-permute-done | bytes 524320 | tf_op jit(solution)/shard_map/ppermute | solution.py:16
  277.8 0.8 copy.17
Async XLA Ops:
  7.2 126.9 %copy-start = (bf16[1,2,192,2048]{3,2,1,0:T(8,128)(2,1)S(1)}, bf16[1,2,192,2048]{3,2,1,0:T(8,128)(2,1)}, u32[]{:S(2)}) copy-start(bf16[1,2,192,2048]{3,2,1,0:T(8,128)(2,1)} %param.13) | copy-start | bytes 4718596
  7.2 254.8 %reduce-scatter.2.cloned.1.call-start = ((), (), s32[]{:S(2)}) async-start(), calls=%async_computation.1 | async-start | bytes 8912896 | tf_op jit(solution)/shard_map/reduce_scatter | solution.py:194
  134.0 6.0 %copy-start.1 = (bf16[1,2,192,2048]{3,2,1,0:T(8,128)(2,1)S(1)}, bf16[1,2,192,2048]{3,2,1,0:T(8,128)(2,1)}, u32[]{:S(2)}) copy-start(bf16[1,2,192,2048]{3,2,1,0:T(8,128)(2,1)} %param.12) | copy-start | bytes 4718596
  140.0 9.8 %copy-start.5 = (bf16[1,2,192,2048]{3,2,1,0:T(8,128)(2,1)S(1)}, bf16[1,2,192,2048]{3,2,1,0:T(8,128)(2,1)}, u32[]{:S(2)}) copy-start(bf16[1,2,192,2048]{3,2,1,0:T(8,128)(2,1)} %param.11) | copy-start | bytes 4718596
  148.1 1.1 copy-start.2
  148.2 1.7 copy-start.4
  158.8 8.6 %copy-start.3 = (bf16[2048,384]{0,1:T(8,128)(2,1)S(1)}, bf16[2048,384]{0,1:T(8,128)(2,1)}, u32[]{:S(2)}) copy-start(bf16[2048,384]{0,1:T(8,128)(2,1)} %copy-done.2) | copy-start | bytes 4718596
  262.0 15.8 %collective-permute-start = (bf16[128,2048]{1,0:T(8,128)(2,1)}, bf16[128,2048]{1,0:T(8,128)(2,1)S(1)}, u32[]{:S(2)}, u32[]{:S(2)}) collective-permute-start(bf16[128,2048]{1,0:T(8,128)(2,1)} %reduce-scatter.2.cloned.1.call-done), channel_id=1, source_target_pairs={{1,0},{3,2},{5,4},{7,6},{9,8},{11,10},{13,12},{15,14},{17,16},{19,... | collective-permute-start | bytes 1572872 | tf_op jit(solution)/shard_map/ppermute | solution.py:16
Sparse Core Ops, SparseCore 0:
  158.9 102.9 reduce-scatter.1

commit v2 on v1

--- a/solution.py
+++ b/solution.py
@@ -32,6 +32,7 @@
 def gather_kernel(ways, lines, *refs):
     count = (len(refs) - 3) // 2
     own, full = refs[:count], refs[count : 2 * count]
+    pieces = pieces_of(own)
     send_sem, recv_sem, local_sem = refs[2 * count :]
     dp, z = lax.axis_index("dp"), lax.axis_index("expert")
     across = lax.rem(dp + 2, lines)
@@ -58,16 +59,18 @@
 
     def copy(i, line, place, number, d, e, from_own=False):
         slot = line * ways + place
+        which, start, rows, _ = pieces[i]
+        span = pl.ds(start, rows)
         return pltpu.make_async_remote_copy(
-            src_ref=own[i] if from_own else full[i].at[slot],
-            dst_ref=full[i].at[slot],
+            src_ref=own[which].at[span] if from_own else full[which].at[slot, span],
+            dst_ref=full[which].at[slot, span],
             send_sem=send_sem.at[i, number],
             recv_sem=recv_sem.at[i, slot],
             device_id=target(d, e),
             device_id_type=pl.DeviceIdType.MESH,
         )
 
-    everything = range(count)
+    everything = range(len(pieces))
     pending = []
 
     def send(cond, i, line, place, number, d, e, from_own=False):
@@ -82,14 +85,15 @@
         copy(i, line, place, 0, across, z).wait_recv()
 
     steps = [(0, 0)] + [(j, sign) for j in range(1, ways) for sign in (-1, 1)]
-    kept = [pltpu.make_async_copy(own[i], full[i].at[dp * ways + z], local_sem.at[i]) for i in everything]
+    kept = [pltpu.make_async_copy(own[i], full[i].at[dp * ways + z], local_sem.at[i]) for i in range(count)]
     for i in everything:
         send(z < ways - 1, i, dp, z, 0, dp, up, True)
         send(z > 0, i, dp, z, ways, dp, down, True)
         send(None, i, dp, z, 2 * ways, across, z, True)
     for i in everything:
         send(None, i, dp, z, 4 * ways, beside, z, True)
-        kept[i].start()
+    for k in kept:
+        k.start()
     wide = 2 * ways
     for n, (j, sign) in enumerate(steps):
         if n > 0:
@@ -107,10 +111,11 @@
                         send(jnp.logical_and(here, z < ways - 1), i, dp, place, j, dp, up)
                 elif j < ways - 1:
                     send(jnp.logical_and(here, z > 0), i, dp, place, ways + j, dp, down)
-                send(here, i, dp, place, wide + number, across, z)
+                if not pieces[i][3]:
+                    send(here, i, dp, place, wide + number, across, z)
                 send(here, i, dp, place, 2 * wide + number, beside, z)
-            cross_from(steps[n - 1], z, ways, everything, received, send, across, beside, 3 * wide + n - 1)
-    cross_from(steps[-1], z, ways, everything, received, send, across, beside, 3 * wide + len(steps) - 1)
+            cross_from(steps[n - 1], z, ways, pieces, received, send, across, beside, dp, 3 * wide, n - 1)
+    cross_from(steps[-1], z, ways, pieces, received, send, across, beside, dp, 3 * wide, len(steps) - 1)
     other = lax.rem(beside + 2, lines)
     for line in (beside, other):
         for place in range(ways):
@@ -125,16 +130,38 @@
         k.wait()
 
 
-def cross_from(step, z, ways, everything, received, send, across, beside, number):
+def cross_from(step, z, ways, pieces, received, send, across, beside, dp, base, number):
     j, sign = step
     here = None if j == 0 else (z >= j if sign < 0 else z + j < ways)
     place = lax.rem(z + sign * j + ways, ways)
-    for i in everything:
+    for i, piece in enumerate(pieces):
         if here is None:
             received(i, across, place)
         else:
             pl.when(here)(lambda i=i: received(i, across, place))
-        send(here, i, across, place, number, beside, z)
+        if piece[3] and j < ways - 1:
+            sure = j == 0
+            if sure or sign < 0:
+                rising = z < ways - 1
+                rising = rising if sure else jnp.logical_and(here, rising)
+                send(rising, i, across, place, 2 * ways + 1 + j, dp, lax.rem(z + 1, ways))
+            if sure or sign > 0:
+                falling = z > 0
+                falling = falling if sure else jnp.logical_and(here, falling)
+                send(falling, i, across, place, 3 * ways + j, dp, lax.rem(z + ways - 1, ways))
+        send(here, i, across, place, base + number, beside, z)
+
+
+def pieces_of(blocks):
+    pieces = []
+    for i, block in enumerate(blocks):
+        rows, early = block.shape[0], 16
+        if i == 0 or rows <= early:
+            pieces.append((i, 0, rows, False))
+        else:
+            pieces.append((i, 0, rows - early, False))
+            pieces.append((i, rows - early, early, True))
+    return pieces
 
 
 def gathered(*blocks):
@@ -146,8 +173,8 @@
         in_specs=[pl.BlockSpec(memory_space=pl.ANY)] * len(blocks),
         out_specs=[pl.BlockSpec(memory_space=pl.ANY)] * len(blocks),
         scratch_shapes=[
-            pltpu.SemaphoreType.DMA((len(blocks), 8 * ways)),
-            pltpu.SemaphoreType.DMA((len(blocks), slots)),
+            pltpu.SemaphoreType.DMA((len(pieces_of(blocks)), 8 * ways)),
+            pltpu.SemaphoreType.DMA((len(pieces_of(blocks)), slots)),
             pltpu.SemaphoreType.DMA((len(blocks),)),
         ],
         compiler_params=pltpu.CompilerParams(collective_id=0, has_side_effects=True),

time: 286 us -> 279 us (0.976)
  Pallas kernels: 117 us -> 111 us
    pallas_call x1, Pallas kernels: 117 us -> 111 us  [gathered(): pl.pallas_call(functools.partial(gather_kernel, ways, lines), out_shape=[...]
where the time goes in v2:
time: 279 us
  Pallas kernels  111 us (40%)
  waiting for transfers between devices  92.5 us (33%)
  matrix products  54.5 us (20%)
  between operations  14.1 us (5%)
  local copies, waits for them, and re-layouts  5.1 us (2%)
    pallas_call x1, Pallas kernels, gathered(): pl.pallas_call(functools.partial(gather_kernel, ways, lines), out_shape=[...  111 us
    reduce_scatter x1, waiting for transfers between devices, body(): lax.psum_scatter(partial_value.astype(jnp.bfloat16), GROUP, scatter_dimen...  85.9 us
    dot_general x3, matrix products, over_rows(): lax.dot_general(a, b, (((0,), (0,)), ((), ())), preferred_element_type=jn...  25.1 us
    dot_general x3, matrix products, rows_by(): lax.dot_general(a, b, (((1,), (1,)), ((), ())), preferred_element_type=jn...  20.4 us
    dot_general x1, matrix products, body(): partial_value = jnp.dot(deltas, mats, preferred_element_type=jnp.float32)  8.98 us
    ppermute x1, waiting for transfers between devices, passed_along(): return lax.ppermute(block, axis, route)  6.61 us
  transfers between devices with their start and end apart: 2, of which 2 were waited for; matrix products, arithmetic and copies ran while one was open for 9% of the time, Pallas kernels for 0%

profile of v2, /device:TPU:0, one launch (start us, length us, event | category | flops | bytes accessed | tf_op | source)
XLA Modules:
  0.0 279.2 jit_solution(8249237309048002979)
XLA Ops:
  7.2 0.0 copy-start
  7.2 0.0 reduce-scatter.2.cloned.1.call-start
  7.2 0.8 select_reduce_fusion
  8.1 0.1 copy.14
  8.2 0.6 pad.4.refs_0_
  8.8 110.8 %shard_map.102 = (f32[16,128,128]{2,1,0:T(8,128)}, bf16[16,128,2048]{2,1,0:T(8,128)(2,1)}, bf16[16,128,2048]{2,1,0:T(8,128)(2,1)}) custom-call(f32[128,128]{1,0:T(8,128)} %pad.4.refs_0_, bf16[128,2048]{1,0:T(8,128)(2,1)} %bitcast.41, bf16[128,2048]{1,0:T(8,128)(2,1)} %bitcast.42), custom_call_target="tpu_custom_call" | custom-call | tf_op jit(solution)/shard_map/pallas_call | solution.py:170
  119.6 1.6 constant_dynamic-slice_fusion
  121.2 0.3 copy.15
  121.5 6.4 %fusion.9 = f32[2048,384]{0,1:T(8,128)S(1)} fusion(bf16[2048,2048]{1,0:T(8,128)(2,1)} %bitcast.34, bf16[384,2048]{1,0:T(8,128)(2,1)} %bitcast.46), kind=kOutput, calls=%fused_computation.21 | convolution fusion | flops 3221225472 | bytes 13107200 | tf_op jit(solution)/shard_map/dot_general | solution.py:20
  127.9 0.0 copy-done
  127.9 0.0 copy-start.1
  127.9 6.0 %bitcast_multiply_fusion.1 = f32[2048,384]{0,1:T(8,128)S(1)} fusion(bf16[2048,2048]{1,0:T(8,128)(2,1)} %bitcast.32, bf16[384,2048]{1,0:T(8,128)(2,1)S(1)} %bitcast.31, f32[2048,2]{0,1:T(2,128)S(1)} %copy.15), kind=kOutput, calls=%fused_computation.2 | convolution fusion | flops 3222011904 | bytes 13123584 | tf_op jit(solution)/shard_map/dot_general | solution.py:20
  133.9 0.0 copy-done.1
  133.9 0.0 copy-start.5
  133.9 8.1 %fusion = (bf16[2048,384]{0,1:T(8,128)(2,1)S(1)}, bf16[2048,384]{0,1:T(8,128)(2,1)S(1)}, bf16[2048,384]{0,1:T(8,128)(2,1)S(1)}) fusion(f32[2048,2]{0,1:T(2,128)S(1)} %copy.15, f32[2048,384]{0,1:T(8,128)S(1)} %fusion.9, f32[2048,384]{0,1:T(8,128)S(1)} %bitcast_multiply_fusion.1, bf16[2048,2048]{1,0:T(8,128)(2,1)} %bitcast.35, bf16[384,2048]{1,0:T(8,128)(2,1)S(1)} %bitcast.38), kind=kOutput, calls=%fused_computation.3 | convolution fusion | flops 3233808384 | bytes 20987904 | tf_op jit(solution)/shard_map/dot_general | solution.py:20
  142.0 0.0 copy-start.2
  142.0 0.0 copy-start.4
  142.0 1.1 copy-done.2
  143.1 0.5 copy-done.4
  143.6 0.0 copy-done.5
  143.6 9.0 %convolution_convert_fusion = bf16[2048,2048]{1,0:T(8,128)(2,1)} fusion(bf16[2048,384]{0,1:T(8,128)(2,1)S(1)} %get-tuple-element.12, bf16[2048,384]{0,1:T(8,128)(2,1)S(1)} %get-tuple-element.11, bf16[384,2048]{1,0:T(8,128)(2,1)S(1)} %bitcast.39, bf16[384,2048]{1,0:T(8,128)(2,1)S(1)} %bitcast.47), kind=kOutput, calls=%fused_computation | convolution fusion | flops 6459228160 | bytes 14680064 | tf_op jit(solution)/shard_map/dot_general | solution.py:220
  152.6 0.0 reduce-scatter.2.cloned.1.call-update
  152.7 0.0 copy-start.3
  152.7 8.6 %convolution_convert_fusion.3 = bf16[384,2048]{1,0:T(8,128)(2,1)} fusion(bf16[2048,384]{0,1:T(8,128)(2,1)} %copy-done.4, bf16[2048,2048]{1,0:T(8,128)(2,1)} %bitcast.36), kind=kOutput, calls=%fused_computation.16 | convolution fusion | flops 3222011904 | bytes 11534336 | tf_op jit(solution)/shard_map/dot_general | solution.py:24
  161.2 0.0 copy-done.3
  161.2 8.7 %convolution_convert_fusion.2 = bf16[384,2048]{1,0:T(8,128)(2,1)} fusion(bf16[2048,384]{0,1:T(8,128)(2,1)S(1)} %copy-done.3, bf16[2048,2048]{1,0:T(8,128)(2,1)} %bitcast.37), kind=kOutput, calls=%fused_computation.15 | convolution fusion | flops 3222011904 | bytes 11534336 | tf_op jit(solution)/shard_map/dot_general | solution.py:24
  169.9 85.9 %reduce-scatter.2.cloned.1.call-done = bf16[128,2048]{1,0:T(8,128)(2,1)} async-done(((bf16[2048,2048]{1,0:T(8,128)(2,1)}), bf16[128,2048]{1,0:T(8,128)(2,1)}) %reduce-scatter.2.cloned.1.call-update) | async-done | bytes 524304 | tf_op jit(solution)/shard_map/reduce_scatter | solution.py:221
  255.8 1.3 collective-permute-start
  257.1 7.9 %convolution_convert_fusion.1 = bf16[384,2048]{1,0:T(8,128)(2,1)} fusion(bf16[2048,384]{0,1:T(8,128)(2,1)S(1)} %get-tuple-element.10, bf16[2048,2048]{1,0:T(8,128)(2,1)} %bitcast.33), kind=kOutput, calls=%fused_computation.14 | convolution fusion | flops 3222011904 | bytes 11534336 | tf_op jit(solution)/shard_map/dot_general | solution.py:24
  265.0 6.6 %collective-permute-done = bf16[128,2048]{1,0:T(8,128)(2,1)S(1)} collective-permute-done((bf16[128,2048]{1,0:T(8,128)(2,1)}, bf16[128,2048]{1,0:T(8,128)(2,1)S(1)}, u32[]{:S(2)}, u32[]{:S(2)}) %collective-permute-start) | collective-permute-done | bytes 524320 | tf_op jit(solution)/shard_map/ppermute | solution.py:16
  271.6 0.8 copy.17
Async XLA Ops:
  7.2 120.7 %copy-start = (bf16[1,2,192,2048]{3,2,1,0:T(8,128)(2,1)S(1)}, bf16[1,2,192,2048]{3,2,1,0:T(8,128)(2,1)}, u32[]{:S(2)}) copy-start(bf16[1,2,192,2048]{3,2,1,0:T(8,128)(2,1)} %param.13) | copy-start | bytes 4718596
  7.2 248.6 %reduce-scatter.2.cloned.1.call-start = ((), (), s32[]{:S(2)}) async-start(), calls=%async_computation.1 | async-start | bytes 8912896 | tf_op jit(solution)/shard_map/reduce_scatter | solution.py:221
  127.9 6.0 %copy-start.1 = (bf16[1,2,192,2048]{3,2,1,0:T(8,128)(2,1)S(1)}, bf16[1,2,192,2048]{3,2,1,0:T(8,128)(2,1)}, u32[]{:S(2)}) copy-start(bf16[1,2,192,2048]{3,2,1,0:T(8,128)(2,1)} %param.12) | copy-start | bytes 4718596
  133.9 9.8 %copy-start.5 = (bf16[1,2,192,2048]{3,2,1,0:T(8,128)(2,1)S(1)}, bf16[1,2,192,2048]{3,2,1,0:T(8,128)(2,1)}, u32[]{:S(2)}) copy-start(bf16[1,2,192,2048]{3,2,1,0:T(8,128)(2,1)} %param.11) | copy-start | bytes 4718596
  142.0 1.1 copy-start.2
  142.0 1.7 copy-start.4
  152.7 8.6 %copy-start.3 = (bf16[2048,384]{0,1:T(8,128)(2,1)S(1)}, bf16[2048,384]{0,1:T(8,128)(2,1)}, u32[]{:S(2)}) copy-start(bf16[2048,384]{0,1:T(8,128)(2,1)} %copy-done.2) | copy-start | bytes 4718596
  255.8 15.8 %collective-permute-start = (bf16[128,2048]{1,0:T(8,128)(2,1)}, bf16[128,2048]{1,0:T(8,128)(2,1)S(1)}, u32[]{:S(2)}, u32[]{:S(2)}) collective-permute-start(bf16[128,2048]{1,0:T(8,128)(2,1)} %reduce-scatter.2.cloned.1.call-done), channel_id=1, source_target_pairs={{1,0},{3,2},{5,4},{7,6},{9,8},{11,10},{13,12},{15,14},{17,16},{19,... | collective-permute-start | bytes 1572872 | tf_op jit(solution)/shard_map/ppermute | solution.py:16
Sparse Core Ops, SparseCore 0:
  152.8 102.9 reduce-scatter.1
